TPU v7x, 32 devices: a whole 2x2x4 slice. The times are simulated.
32 devices in a mesh: groups: 2 (over y), gx: 16 (over z, x, core).
Axes of the slice: x: 2, y: 2, z: 4, core: 2. Of those that a mesh axis runs over, the one named last changes fastest.
Arguments:
- tokens: bfloat16 [3, 32, 18432], P(None, ('groups', 'gx')), parts along dimension 1, may hold values from -150 to 150
- gain: float32 [18432], replicated, may hold values from 0.5 to 1.5
- w_query: bfloat16 [18432, 12288], P(None, 'gx'), may hold values from -0.046875 to 0.046875
- w_key: bfloat16 [18432, 256], P(None, 'gx'), may hold values from -0.25 to 0.25
- w_value: bfloat16 [18432, 256], P(None, 'gx'), may hold values from -0.046875 to 0.046875
- w_out: bfloat16 [12288, 18432], P(None, 'gx'), may hold values from -0.0546875 to 0.0546875
- cache_keys: bfloat16 [32, 2048, 256], P(('groups', 'gx')), parts along dimension 0, may hold values from -690 to 690
- cache_values: bfloat16 [32, 2048, 256], P(('groups', 'gx')), parts along dimension 0, may hold values from -24 to 24
- lengths: int32 [32], P(('groups', 'gx')), parts along dimension 0, may hold values from 16 to 2048, as said below
- positions: int32 [32], P(('groups', 'gx')), parts along dimension 0, may hold values from 0 to 4095
Outputs:
- layer_out: bfloat16 [3, 32, 18432], P(None, ('groups', 'gx')), parts along dimension 1
There are 2 independent parts, one for each index of `groups`. A program takes and returns all parts, laid end to end along the dimension named above; an argument that names none is the same for every part. Nothing has to cross between parts.
Inputs may be any that keep to these rules, and one draw needn't show every extreme that they name: `lengths`: at least 16 live slots in every row; in every draw some row has all 2048 slots live.
All inputs are finite; a program needn't handle non-finite values.
Results may differ from a plain program's by a relative error of at most 0.0075.
The roundings to bfloat16 on the way count: a program that leaves them out, or rounds other values in their place, can miss the bound.
Values may be sent and summed in bfloat16 or wider, within the bound.
A program may use at most 192 MiB of HBM per device.

v0:
```python
import jax
import jax.numpy as jnp
from jax import lax
from jax.sharding import PartitionSpec as P


def rotate(values, where):
    half = values.shape[-1] // 2
    freq = 10000.0 ** (-jnp.arange(half, dtype=jnp.float32) * 2.0 / values.shape[-1])
    angle = where[..., None] * freq
    cosine = jnp.cos(angle)
    sine = jnp.sin(angle)
    first_half = values[..., :half]
    second_half = values[..., half:]
    return jnp.concatenate(
        [first_half * cosine - second_half * sine, second_half * cosine + first_half * sine],
        axis=-1,
    )


def per_device(
    tokens, gain, w_query, w_key, w_value, w_out, cache_keys, cache_values, lengths, positions
):
    step_count, row_count, model_width = tokens.shape
    devices = lax.axis_size("gx")
    query_cols = w_query.shape[1]
    key_cols = w_key.shape[1]
    head_size = cache_keys.shape[2]
    slot_count = cache_keys.shape[1]
    head_count = query_cols * devices // head_size
    scale = 1.0 / head_size**0.5
    row_mean_input = tokens.astype(jnp.float32)
    row_mean = jnp.mean(row_mean_input, axis=-1, keepdims=True)
    row_square = jnp.mean(row_mean_input * row_mean_input, axis=-1, keepdims=True)
    row_spread = row_square - row_mean * row_mean
    normed = ((row_mean_input - row_mean) * lax.rsqrt(row_spread + 1e-06) * gain).astype(
        jnp.bfloat16
    )
    everyone = lax.all_gather(normed, "gx", axis=1, tiled=True)

    def project(weight):
        return jnp.einsum(
            "cbd,de->cbe", everyone, weight, preferred_element_type=jnp.float32
        ).astype(jnp.bfloat16)

    small = jnp.concatenate([project(w_key), project(w_value)], axis=-1)
    query_part = project(w_query)
    together = jnp.concatenate([query_part, small], axis=-1)
    swapped = lax.all_to_all(
        together.reshape(step_count, devices, row_count, -1), "gx", split_axis=1, concat_axis=1
    )
    swapped = jnp.swapaxes(swapped, 1, 2)
    queries = swapped[..., :query_cols].reshape(step_count, row_count, head_count, head_size)
    new_keys = swapped[..., query_cols : query_cols + key_cols].reshape(
        step_count, row_count, head_size
    )
    new_values = swapped[..., query_cols + key_cols :].reshape(step_count, row_count, head_size)
    step_place = (
        positions[None, :].astype(jnp.float32)
        + jnp.arange(step_count).astype(jnp.float32)[:, None]
    )
    rotated_queries = rotate(queries.astype(jnp.float32), step_place[:, :, None]).astype(
        jnp.bfloat16
    )
    rotated_keys = rotate(new_keys.astype(jnp.float32), step_place).astype(jnp.bfloat16)
    live_mask = jnp.arange(slot_count)[None, :] < lengths[:, None]
    cache_scores = (
        jnp.einsum(
            "crhd,rjd->crhj", rotated_queries, cache_keys, preferred_element_type=jnp.float32
        )
        * scale
    )
    cache_scores = jnp.where(live_mask[None, :, None, :], cache_scores, -jnp.inf)
    fresh_scores = (
        jnp.einsum(
            "crhd,trd->crht", rotated_queries, rotated_keys, preferred_element_type=jnp.float32
        )
        * scale
    )
    causal = jnp.arange(step_count)[None, :] <= jnp.arange(step_count)[:, None]
    fresh_scores = jnp.where(causal[:, None, None, :], fresh_scores, -jnp.inf)
    highest = jnp.maximum(jnp.max(cache_scores, axis=-1), jnp.max(fresh_scores, axis=-1))[
        ..., None
    ]
    cache_exp = jnp.exp(cache_scores - highest)
    fresh_exp = jnp.exp(fresh_scores - highest)
    denominator = jnp.sum(cache_exp, axis=-1, keepdims=True) + jnp.sum(
        fresh_exp, axis=-1, keepdims=True
    )
    cache_weights = (cache_exp / denominator).astype(jnp.bfloat16)
    fresh_weights = (fresh_exp / denominator).astype(jnp.bfloat16)
    attended = jnp.einsum(
        "crhj,rjd->crhd", cache_weights, cache_values, preferred_element_type=jnp.float32
    )
    attended = attended + jnp.einsum(
        "crht,trd->crhd", fresh_weights, new_values, preferred_element_type=jnp.float32
    )
    attended = attended.astype(jnp.bfloat16).reshape(
        step_count, row_count, head_count * head_size
    )
    mixed_cols = jnp.einsum(
        "cbq,qd->cbd",
        lax.all_gather(attended, "gx", axis=1, tiled=True),
        w_out,
        preferred_element_type=jnp.float32,
    ).astype(jnp.bfloat16)
    return lax.all_to_all(mixed_cols, "gx", split_axis=1, concat_axis=2, tiled=True)


def solution(mesh):
    in_specs = (
        P(None, ("groups", "gx"), None),
        P(),
        P(None, "gx"),
        P(None, "gx"),
        P(None, "gx"),
        P(None, "gx"),
        P(("groups", "gx"), None, None),
        P(("groups", "gx"), None, None),
        P(("groups", "gx")),
        P(("groups", "gx")),
    )
    out_specs = P(None, ("groups", "gx"), None)
    return jax.shard_map(
        per_device, mesh=mesh, in_specs=in_specs, out_specs=out_specs, check_vma=False
    )
```

profile of v0, /device:TPU:0, one launch (start us, length us, event | category | flops | bytes accessed | tf_op | source)
XLA Modules:
  0.0 159.4 jit_solution(1783965883813707163)
XLA Ops:
  6.5 0.0 copy-start
  6.5 0.0 all-gather.3.cloned.1.call-start
  6.5 1.3 convert_reduce_fusion
  7.8 1.8 %fusion.30 = bf16[3,1,18432]{2,0,1:T(4,128)(2,1)} fusion(bf16[3,1,18432]{2,0,1:T(4,128)(2,1)} %param.10, f32[18432]{0:T(1024)} %param.11, f32[3]{0:T(128)S(1)} %get-tuple-element.16, f32[3]{0:T(128)S(1)} %get-tuple-element.15), kind=kLoop, calls=%fused_computation.37 | loop fusion | flops 276480 | bytes 294936 | tf_op jit(solution)/shard_map/convert_element_type | solution.py:36
  9.6 0.0 all-gather.3.cloned.1.call-update
  10.3 0.1 multiply_cosine_fusion.1
  10.4 0.0 copy-start.4
  10.5 44.4 %all-gather.3.cloned.1.call-done = bf16[3,16,18432]{2,0,1:T(4,128)(2,1)} async-done(((bf16[3,1,18432]{2,0,1:T(4,128)(2,1)}), bf16[3,16,18432]{2,0,1:T(4,128)(2,1)}) %all-gather.3.cloned.1.call-update) | async-done | bytes 1769488 | tf_op jit(solution)/shard_map/all_gather | solution.py:39
  54.8 0.0 copy-start.2
  54.8 15.4 %fusion.12 = bf16[3,16,768]{2,1,0:T(8,128)(2,1)S(1)} fusion(bf16[18432,768]{1,0:T(8,128)(2,1)} %param.12, bf16[3,16,18432]{2,0,1:T(4,128)(2,1)} %all-gather.3.cloned.1.call-done), kind=kOutput, calls=%fused_computation.15 | convolution fusion | flops 1358991360 | bytes 30154752 | tf_op jit(solution)/shard_map/cbd,de->cbe/dot_general | solution.py:42
  70.2 0.0 copy-done.4
  70.2 0.0 copy-done.2
  70.3 0.0 copy-start.5
  70.3 1.4 convolution_convert_fusion
  71.7 0.0 copy-done.5
  71.7 1.4 convolution_convert_fusion.1
  73.2 0.1 maximum_bitcast_fusion
  73.3 0.7 copy.31
  73.9 3.5 %all-to-all-start = ((bf16[3,16,1,800]{3,0,2,1:T(4,128)(2,1)}), bf16[3,16,1,800]{3,0,2,1:T(4,128)(2,1)S(1)}, u32[]{:S(2)}, u32[]{:S(2)}) async-start(bf16[3,16,1,800]{3,0,2,1:T(4,128)(2,1)} %copy.31), calls=%async_computation | async-start | bytes 229376 | tf_op jit(solution)/shard_map/all_to_all | solution.py:49
  77.5 0.2 all-gather.5.cloned.1.call-start
  78.4 6.7 %all-to-all-done = bf16[3,16,1,800]{3,0,2,1:T(4,128)(2,1)S(1)} async-done(((bf16[3,16,1,800]{3,0,2,1:T(4,128)(2,1)}), bf16[3,16,1,800]{3,0,2,1:T(4,128)(2,1)S(1)}, u32[]{:S(2)}, u32[]{:S(2)}) %all-to-all-start) | async-done | bytes 76832 | tf_op jit(solution)/shard_map/all_to_all | solution.py:49
  85.2 0.1 fusion.51
  85.3 0.1 reshape.387
  85.4 0.1 fusion.48
  85.5 0.0 copy-done
  85.5 0.0 copy-start.3
  85.5 0.6 fusion.52
  86.1 0.2 fusion.53
  86.3 0.3 fusion.20
  86.6 0.1 reshape.384
  86.7 0.0 copy-done.3
  86.7 0.4 convolution_bitcast_fusion
  87.1 0.2 fusion.15
  87.4 0.7 reshape.375
  88.1 0.0 all-gather.5.cloned.1.call-update
  88.1 37.4 %all-gather.5.cloned.1.call-done = bf16[3,16,12288]{2,0,1:T(4,128)(2,1)} async-done(((bf16[3,1,12288]{2,0,1:T(4,128)(2,1)}), bf16[3,16,12288]{2,0,1:T(4,128)(2,1)}) %all-gather.5.cloned.1.call-update) | async-done | bytes 1179664 | tf_op jit(solution)/shard_map/all_gather | solution.py:103
  125.5 0.0 copy-start.1
  125.5 14.8 %fusion.7 = bf16[3,16,1152]{2,1,0:T(8,128)(2,1)S(1)} fusion(bf16[12288,1152]{1,0:T(8,128)(2,1)} %param.15, bf16[3,16,12288]{2,0,1:T(4,128)(2,1)} %all-gather.5.cloned.1.call-done), kind=kOutput, calls=%fused_computation.8 | convolution fusion | flops 1359009792 | bytes 29601792 | tf_op jit(solution)/shard_map/cbq,qd->cbd/dot_general | solution.py:101
  140.3 0.1 copy.36
  140.3 11.6 %all_to_all.17 = bf16[3,16,1152]{2,0,1:T(4,128)(2,1)S(1)} all-to-all(bf16[3,16,1152]{2,0,1:T(4,128)(2,1)S(1)} %copy.36), channel_id=1, replica_groups=mesh['groups'=2,'gx'=16] {'gx'}, dimensions={1} | all-to-all | bytes 221184 | tf_op jit(solution)/shard_map/all_to_all | solution.py:107
  151.9 0.7 copy.50
  152.6 0.0 copy-done.1
  (12 shorter events, 0.2 us)
Async XLA Ops:
  6.5 79.0 %copy-start = (bf16[1,2048,256]{2,1,0:T(8,128)(2,1)S(1)}, bf16[1,2048,256]{2,1,0:T(8,128)(2,1)}, u32[]{:S(2)}) copy-start(bf16[1,2048,256]{2,1,0:T(8,128)(2,1)} %param.16) | copy-start | bytes 3145732
  6.5 48.3 %all-gather.3.cloned.1.call-start = ((), (), s32[]{:S(2)}) async-start(), calls=%async_computation.2 | async-start | bytes 2506752 | tf_op jit(solution)/shard_map/all_gather | solution.py:39
  10.4 59.8 %copy-start.4 = (bf16[18432,16]{0,1:T(8,128)(2,1)S(1)}, bf16[18432,16]{0,1:T(8,128)(2,1)}, u32[]{:S(2)}) copy-start(bf16[18432,16]{0,1:T(8,128)(2,1)} %param.14) | copy-start | bytes 1769476
  54.8 15.4 %copy-start.2 = (bf16[3,16,18432]{2,0,1:T(4,128)(2,1)S(1)}, bf16[3,16,18432]{2,0,1:T(4,128)(2,1)}, u32[]{:S(2)}) copy-start(bf16[3,16,18432]{2,0,1:T(4,128)(2,1)} %all-gather.3.cloned.1.call-done) | copy-start | bytes 5308420
  70.3 1.4 copy-start.5
  73.9 11.2 %all-to-all-start = ((bf16[3,16,1,800]{3,0,2,1:T(4,128)(2,1)}), bf16[3,16,1,800]{3,0,2,1:T(4,128)(2,1)S(1)}, u32[]{:S(2)}, u32[]{:S(2)}) async-start(bf16[3,16,1,800]{3,0,2,1:T(4,128)(2,1)} %copy.31), calls=%async_computation | async-start | bytes 229376 | tf_op jit(solution)/shard_map/all_to_all | solution.py:49
  77.5 48.0 %all-gather.5.cloned.1.call-start = ((), (), s32[]{:S(2)}) async-start(), calls=%async_computation.3 | async-start | bytes 1671168 | tf_op jit(solution)/shard_map/all_gather | solution.py:103
  85.5 1.2 copy-start.3
  125.5 27.1 %copy-start.1 = (bf16[1,2048,256]{2,1,0:T(8,128)(2,1)S(1)}, bf16[1,2048,256]{2,1,0:T(8,128)(2,1)}, u32[]{:S(2)}) copy-start(bf16[1,2048,256]{2,1,0:T(8,128)(2,1)} %param.16) | copy-start | bytes 3145732
Sparse Core Ops, SparseCore 0:
  9.8 45.0 all-gather.2
  88.2 37.2 all-gather.4
where the time goes:
time: 160 us; the launch traced here: 159 us
  waiting for transfers between devices  88.5 us (55%)
  matrix products  34.4 us (22%)
  between operations  14.9 us (9%)
  blocking collectives  11.6 us (7%)
  other arithmetic  3.89 us (2%)
  starting transfers between devices  3.74 us (2%)
  local copies, waits for them, and re-layouts  2.36 us (1%)
    all_gather x1, waiting for transfers between devices, per_device(): everyone = lax.all_gather(normed, 'gx', axis=1, tiled=True)  44.4 us
    all_gather x1, waiting for transfers between devices, per_device(): lax.all_gather(attended, 'gx', axis=1, tiled=True)  37.4 us
    dot_general x3, matrix products, project(): jnp.einsum('cbd,de->cbe', everyone, weight, preferred_element_type=jnp.fl...  18.3 us
    dot_general x1, matrix products, per_device(): jnp.einsum('cbq,qd->cbd', lax.all_gather(attended, 'gx', axis=1, tiled=Tr...  14.8 us
    all_to_all x1, blocking collectives, per_device(): lax.all_to_all(mixed_cols, 'gx', split_axis=1, concat_axis=2, tiled=True)  11.6 us
    all_to_all x1, waiting for transfers between devices, per_device(): lax.all_to_all(together.reshape(step_count, devices, row_count, -1), 'gx'...  6.75 us
    all_to_all x1, starting transfers between devices, per_device(): lax.all_to_all(together.reshape(step_count, devices, row_count, -1), 'gx'...  3.51 us
  transfers between devices with their start and end apart: 3, of which 3 were waited for; matrix products, arithmetic and copies ran while one was open for 0% of the time, Pallas kernels for 0%

commit v1 on v0

--- a/solution.py
+++ b/solution.py
@@ -1,6 +1,8 @@
 import jax
 import jax.numpy as jnp
 from jax import lax
+from jax.experimental import pallas as pl
+from jax.experimental.pallas import tpu as pltpu
 from jax.sharding import PartitionSpec as P
 
 
@@ -18,7 +20,7 @@
     )
 
 
-def per_device(
+def plain_layer(
     tokens, gain, w_query, w_key, w_value, w_out, cache_keys, cache_values, lengths, positions
 ):
     step_count, row_count, model_width = tokens.shape
@@ -107,6 +109,510 @@
     return lax.all_to_all(mixed_cols, "gx", split_axis=1, concat_axis=2, tiled=True)
 
 
+MESH = pl.DeviceIdType.MESH
+PEERS = 16
+VMEM_BYTES = 64 * 1024 * 1024
+PARTS = 3
+ACROSS, SIBLING = range(2)
+
+
+def layer_kernel(
+    tokens,
+    gain,
+    lengths,
+    positions,
+    wq_hbm,
+    wk_hbm,
+    wv_hbm,
+    wo_hbm,
+    keys_hbm,
+    values_hbm,
+    out,
+    wq,
+    wkv,
+    wo,
+    keys,
+    values,
+    blocks,
+    left,
+    spread,
+    moved,
+    acc,
+    out_acc,
+    rotated,
+    sent,
+    got,
+    sent_out,
+    got_out,
+    wq_sem,
+    wkv_sem,
+    wo_sem,
+    cache_sem,
+    line_sem,
+    send_sem,
+    recv_sem,
+    swap_send,
+    swap_recv,
+    back_send,
+    back_recv,
+):
+    f32 = jnp.float32
+    bf16 = jnp.bfloat16
+    steps = 3
+    me = lax.axis_index("gx")
+    z, x, core = me // 4, (me // 2) % 2, me % 2
+
+    def at(zz, xx, cc):
+        return zz * 4 + xx * 2 + cc
+
+    wq_copies = [
+        pltpu.make_async_copy(wq_hbm.at[c], wq.at[c], wq_sem.at[c]) for c in range(PARTS)
+    ]
+    part_len = wkv.shape[2]
+    wkv_copies = []
+    for c in range(PARTS):
+        cols = pl.ds(c * part_len, part_len)
+        wkv_copies.append(
+            (
+                pltpu.make_async_copy(
+                    wk_hbm.at[:, cols], wkv.at[c, pl.ds(0, 16), :], wkv_sem.at[c, 0]
+                ),
+                pltpu.make_async_copy(
+                    wv_hbm.at[:, cols], wkv.at[c, pl.ds(16, 16), :], wkv_sem.at[c, 1]
+                ),
+            )
+        )
+    wo_copies = [
+        pltpu.make_async_copy(wo_hbm.at[:, c], wo.at[c], wo_sem.at[c]) for c in range(PARTS)
+    ]
+    keys_copy = pltpu.make_async_copy(keys_hbm, keys, cache_sem.at[0])
+    values_copy = pltpu.make_async_copy(values_hbm, values, cache_sem.at[1])
+    for c in range(PARTS):
+        wq_copies[c].start()
+        wkv_copies[c][0].start()
+        wkv_copies[c][1].start()
+    keys_copy.start()
+    values_copy.start()
+    for c in range(PARTS):
+        wo_copies[c].start()
+
+    barrier = pltpu.get_barrier_semaphore()
+    for shift in range(1, PEERS):
+        pl.semaphore_signal(
+            barrier, inc=1, device_id={"gx": (me + shift) % PEERS}, device_id_type=MESH
+        )
+
+    width = blocks.shape[3]
+    features = PARTS * 16 * width
+    raw = tokens[...].astype(f32)
+    mean = jnp.sum(raw, axis=1, keepdims=True) * (1.0 / features)
+    square = jnp.sum(raw * raw, axis=1, keepdims=True) * (1.0 / features)
+    factor = lax.rsqrt(square - mean * mean + 1e-06)
+    for c in range(PARTS):
+        for u in range(16):
+            for group in range(width // 128):
+                cols = pl.ds((c * 16 + u) * width + group * 128, 128)
+                line = (tokens[:, cols].astype(f32) - mean) * factor * gain[:, cols]
+                spread[group, pl.ds(u, steps, 16), :] = line
+        for group in range(width // 128):
+            blocks[c, me, :, pl.ds(group * 128, 128)] = spread[group, pl.ds(0, 48), :].astype(
+                bf16
+            )
+
+    pl.semaphore_wait(barrier, PEERS - 1)
+
+    def gather(lanes):
+        def copy(c, d, sem, target):
+            ref = blocks.at[c, d, :, pl.ds(0, lanes)]
+            return pltpu.make_async_remote_copy(
+                src_ref=ref,
+                dst_ref=ref,
+                send_sem=sem,
+                recv_sem=recv_sem.at[c, d],
+                device_id={"gx": target},
+                device_id_type=MESH,
+            )
+
+        def up(c, k):
+            return copy(c, me, line_sem.at[c, k - 1], at(jnp.minimum(z + k, 3), x, core))
+
+        def down(c, k):
+            return copy(c, me, line_sem.at[c, k + 2], at(jnp.maximum(z - k, 0), x, core))
+
+        def across(c, d):
+            return copy(c, d, send_sem.at[c, ACROSS, d], at(z, 1 - x, core))
+
+        def sibling(c, d):
+            return copy(c, d, send_sem.at[c, SIBLING, d], at(z, x, 1 - core))
+
+        def own(c):
+            for k in range(1, 4):
+                pl.when(z + k <= 3)(up(c, k).start)
+                pl.when(z >= k)(down(c, k).start)
+            across(c, me).start()
+            sibling(c, me).start()
+
+        def hop(c):
+            for k in range(1, 4):
+                for near, d in ((z >= k, at(z - k, x, core)), (z + k <= 3, at(z + k, x, core))):
+
+                    @pl.when(near)
+                    def _(d=d):
+                        sibling(c, d).wait_recv()
+                        across(c, d).start()
+                        sibling(c, d).start()
+
+        def from_across(c):
+            for zz in range(4):
+                d = at(zz, 1 - x, core)
+                sibling(c, d).wait_recv()
+                sibling(c, d).start()
+
+        def from_sibling(c):
+            for zz in range(4):
+                for xx in range(2):
+                    sibling(c, at(zz, xx, 1 - core)).wait_recv()
+
+        def drain(c):
+            for k in range(1, 4):
+                pl.when(z + k <= 3)(up(c, k).wait_send)
+                pl.when(z >= k)(down(c, k).wait_send)
+            for zz in range(4):
+                mine = at(zz, x, core)
+                across(c, mine).wait_send()
+                sibling(c, mine).wait_send()
+                sibling(c, at(zz, 1 - x, core)).wait_send()
+
+        return own, hop, from_across, from_sibling, drain
+
+    def line_up(c, lanes):
+        for t in range(steps):
+            for group in range(lanes // 128):
+                slot = (t * (lanes // 128) + group) % spread.shape[0]
+                cols = pl.ds(group * 128, 128)
+                spread[slot] = (
+                    blocks[c, :, pl.ds(t * 16, 16), cols].astype(f32).reshape(PEERS * 16, 128)
+                )
+                for u in range(16):
+                    left[pl.ds(t * 16, 16), pl.ds(u * lanes + group * 128, 128)] = spread[
+                        slot, pl.ds(u, PEERS, 16), :
+                    ].astype(bf16)
+
+    own, hop, from_across, from_sibling, drain = gather(width)
+    own(0)
+    own(1)
+    own(2)
+    hop(0)
+    hop(1)
+    from_across(0)
+    hop(2)
+    from_across(1)
+    tile = 768
+    acc_q = jnp.zeros(acc.shape, f32)
+    acc_kv = jnp.zeros((48, 32), f32)
+    for c in range(PARTS):
+        if c == 1:
+            from_across(2)
+        from_sibling(c)
+        line_up(c, width)
+        wq_copies[c].wait()
+        wkv_copies[c][0].wait()
+        wkv_copies[c][1].wait()
+
+        def project(i, carry, c=c):
+            acc_q, acc_kv = carry
+            span = pl.ds(pl.multiple_of(i * tile, tile), tile)
+            part = left[:, span]
+            acc_q = acc_q + jnp.dot(part, wq[c, span, :], preferred_element_type=f32)
+            acc_kv = acc_kv + lax.dot_general(
+                part, wkv[c, :, span], (((1,), (1,)), ((), ())), preferred_element_type=f32
+            )
+            return acc_q, acc_kv
+
+        acc_q, acc_kv = lax.fori_loop(0, part_len // tile, project, (acc_q, acc_kv))
+    for c in range(PARTS):
+        drain(c)
+
+    acc[...] = acc_q
+    place_row = lax.broadcasted_iota(jnp.int32, (32, 256), 0)
+    place_col = lax.broadcasted_iota(jnp.int32, (32, 256), 1)
+    small = acc_kv.astype(bf16)
+    place_k = (place_col == me * 16 + place_row) & (place_row < 16)
+    place_v = (place_col == me * 16 + place_row - 16) & (place_row >= 16)
+    full_k = jnp.dot(
+        small, place_k.astype(f32).astype(bf16), preferred_element_type=f32
+    )
+    full_v = jnp.dot(
+        small, place_v.astype(f32).astype(bf16), preferred_element_type=f32
+    )
+    for half in range(2):
+        base = half * 256
+        for t in range(steps):
+            rows = slice(t * 16, t * 16 + 16)
+            for h in range(3):
+                moved[pl.ds(base + t * 3 + h, 16, 16), :] = acc[
+                    rows, pl.ds(h * 256 + half * 128, 128)
+                ]
+            cols = slice(half * 128, half * 128 + 128)
+            moved[pl.ds(base + 9 + t, 16, 16), :] = full_k[rows, cols]
+            moved[pl.ds(base + 12 + t, 16, 16), :] = full_v[rows, cols]
+        moved[pl.ds(base + 15, 16, 16), :] = jnp.zeros((16, 128), f32)
+    for half in range(2):
+        sent[:, :, pl.ds(half * 128, 128)] = (
+            moved[pl.ds(half * 256, 256), :].reshape(PEERS, 16, 128).astype(bf16)
+        )
+
+    def swap(source, target, send_sems, recv_sems, shift):
+        to = (me + shift) % PEERS
+        origin = (me + PEERS - shift) % PEERS
+        out_copy = pltpu.make_async_remote_copy(
+            src_ref=source.at[to],
+            dst_ref=target.at[me],
+            send_sem=send_sems.at[shift],
+            recv_sem=recv_sems.at[shift],
+            device_id={"gx": to},
+            device_id_type=MESH,
+        )
+        in_copy = pltpu.make_async_remote_copy(
+            src_ref=source.at[to],
+            dst_ref=target.at[origin],
+            send_sem=send_sems.at[shift],
+            recv_sem=recv_sems.at[shift],
+            device_id={"gx": to},
+            device_id_type=MESH,
+        )
+        return out_copy, in_copy
+
+    swaps = [swap(sent, got, swap_send, swap_recv, shift) for shift in range(1, PEERS)]
+    for out_copy, _ in swaps:
+        out_copy.start()
+    got[me] = sent[me]
+
+    lane = lax.broadcasted_iota(jnp.int32, (8, 128), 1).astype(f32)
+    step = lax.broadcasted_iota(jnp.int32, (8, 128), 0).astype(f32)
+    freq = jnp.exp(lane * (-2.0 / 256.0) * 9.210340371976184)
+    angle = (positions[0].astype(f32) + step) * freq
+    cosine = jnp.cos(angle)
+    sine = jnp.sin(angle)
+    keys_copy.wait()
+    values_copy.wait()
+    for out_copy, in_copy in swaps:
+        in_copy.wait_recv()
+
+    for half in range(2):
+        moved[pl.ds(half * 256, 256), :] = (
+            got[:, :, pl.ds(half * 128, 128)].astype(f32).reshape(256, 128)
+        )
+    key_rows = []
+    value_rows = []
+    for t in range(steps):
+        cos_t = cosine[t : t + 1]
+        sin_t = sine[t : t + 1]
+        for h in range(3):
+            first = moved[pl.ds(t * 3 + h, 16, 16), :]
+            second = moved[pl.ds(256 + t * 3 + h, 16, 16), :]
+            rows = pl.ds(t * 16, 16)
+            rotated[h, rows, pl.ds(0, 128)] = (first * cos_t - second * sin_t).astype(bf16)
+            rotated[h, rows, pl.ds(128, 128)] = (second * cos_t + first * sin_t).astype(bf16)
+        first = jnp.sum(moved[pl.ds(9 + t, 16, 16), :], axis=0, keepdims=True)
+        second = jnp.sum(moved[pl.ds(256 + 9 + t, 16, 16), :], axis=0, keepdims=True)
+        key_rows.append((first * cos_t - second * sin_t, second * cos_t + first * sin_t))
+        value_rows.append(
+            tuple(
+                jnp.sum(moved[pl.ds(base + 12 + t, 16, 16), :], axis=0, keepdims=True)
+                for base in (0, 256)
+            )
+        )
+    place = lax.broadcasted_iota(jnp.int32, (16, 128), 0)
+
+    def stack(rows):
+        halves = []
+        for half in range(2):
+            stacked = jnp.zeros((16, 128), f32)
+            for t in range(steps):
+                stacked = jnp.where(place == t, rows[t][half], stacked)
+            halves.append(stacked)
+        return jnp.concatenate(halves, axis=1).astype(bf16)
+
+    fresh_keys = stack(key_rows)
+    fresh_values = stack(value_rows)
+
+    slots = keys.shape[0]
+    live = lax.broadcasted_iota(jnp.int32, (48, slots), 1) < lengths[0]
+    row_step = lax.broadcasted_iota(jnp.int32, (48, 16), 0) // 16
+    causal = lax.broadcasted_iota(jnp.int32, (48, 16), 1) <= row_step
+    over = (((1,), (1,)), ((), ()))
+
+    def attend(h):
+        query = rotated[h]
+        score = lax.dot_general(query, keys[...], over, preferred_element_type=f32) * 0.0625
+        score = jnp.where(live, score, -jnp.inf)
+        fresh = lax.dot_general(query, fresh_keys, over, preferred_element_type=f32) * 0.0625
+        fresh = jnp.where(causal, fresh, -jnp.inf)
+        highest = jnp.maximum(
+            jnp.max(score, axis=1, keepdims=True), jnp.max(fresh, axis=1, keepdims=True)
+        )
+        score = jnp.exp(score - highest)
+        fresh = jnp.exp(fresh - highest)
+        whole = jnp.sum(score, axis=1, keepdims=True) + jnp.sum(fresh, axis=1, keepdims=True)
+        share = 1.0 / whole
+        result = jnp.dot(
+            (score * share).astype(bf16), values[...], preferred_element_type=f32
+        ) + jnp.dot((fresh * share).astype(bf16), fresh_values, preferred_element_type=f32)
+        blocks[h, me, :, pl.ds(0, 256)] = result.astype(bf16)
+
+    own, hop, from_across, from_sibling, drain = gather(256)
+    attend(0)
+    own(0)
+    attend(1)
+    own(1)
+    attend(2)
+    own(2)
+    hop(0)
+    hop(1)
+    from_across(0)
+    hop(2)
+    from_across(1)
+    depth = 4
+    for c in range(PARTS):
+        if c == 1:
+            from_across(2)
+        from_sibling(c)
+        line_up(c, 256)
+        wo_copies[c].wait()
+
+        def mix(i, carry, c=c):
+            part = left[:, pl.ds(pl.multiple_of(i * depth * 256, 1024), depth * 256)]
+            weight = wo[c, pl.ds(i * depth, depth)].reshape(depth * 256, out_acc.shape[1])
+            out_acc[...] += jnp.dot(part, weight, preferred_element_type=f32)
+            return carry
+
+        if c == 0:
+            out_acc[...] = jnp.zeros(out_acc.shape, f32)
+        lax.fori_loop(0, 16 // depth, mix, 0)
+    for c in range(PARTS):
+        drain(c)
+    for out_copy, _ in swaps:
+        out_copy.wait_send()
+
+    groups = out_acc.shape[1] // 128
+    for t in range(steps):
+        for group in range(groups):
+            moved[pl.ds(t * groups + group, 16, 32), :] = out_acc[
+                pl.ds(t * 16, 16), pl.ds(group * 128, 128)
+            ]
+    for spare in range(steps * groups, 32):
+        moved[pl.ds(spare, 16, 32), :] = jnp.zeros((16, 128), f32)
+    sent_out[...] = moved[...].reshape(PEERS, 32, 128).astype(bf16)
+    backs = [swap(sent_out, got_out, back_send, back_recv, shift) for shift in range(1, PEERS)]
+    for out_copy, _ in backs:
+        out_copy.start()
+    got_out[me] = sent_out[me]
+    for _, in_copy in backs:
+        in_copy.wait_recv()
+    moved[...] = got_out[...].astype(f32).reshape(PEERS * 32, 128)
+    for source in range(PEERS):
+        for group in range(groups):
+            out[:, pl.ds((source * groups + group) * 128, 128)] = moved[
+                pl.ds(source * 32 + group, steps, groups), :
+            ].astype(bf16)
+    for out_copy, _ in backs:
+        out_copy.wait_send()
+
+
+def layer(
+    tokens, gain, w_query, w_key, w_value, w_out, cache_keys, cache_values, lengths, positions
+):
+    step_count, row_count, model_width = tokens.shape
+    devices = lax.axis_size("gx")
+    query_cols = w_query.shape[1]
+    key_cols = w_key.shape[1]
+    out_cols = w_out.shape[1]
+    head_size = cache_keys.shape[2]
+    slot_count = cache_keys.shape[1]
+    fits = (
+        devices == PEERS
+        and (step_count, row_count, head_size) == (3, 1, 256)
+        and (query_cols, key_cols) == (3 * head_size, 16)
+        and out_cols % 128 == 0
+        and step_count * out_cols <= 32 * 128
+        and model_width == devices * out_cols
+        and model_width % (PARTS * 16 * 384) == 0
+        and w_out.shape[0] == devices * query_cols
+    )
+    if not fits:
+        return plain_layer(
+            tokens,
+            gain,
+            w_query,
+            w_key,
+            w_value,
+            w_out,
+            cache_keys,
+            cache_values,
+            lengths,
+            positions,
+        )
+    part_len = model_width // PARTS
+    width = part_len // 16
+    bf16 = jnp.bfloat16
+    f32 = jnp.float32
+    vmem = pl.BlockSpec(memory_space=pltpu.VMEM)
+    smem = pl.BlockSpec(memory_space=pltpu.SMEM)
+    hbm = pl.BlockSpec(memory_space=pl.ANY)
+    dma = pltpu.SemaphoreType.DMA
+    result = pl.pallas_call(
+        layer_kernel,
+        out_shape=jax.ShapeDtypeStruct((step_count, model_width), bf16),
+        in_specs=[vmem, vmem, smem, smem] + [hbm] * 6,
+        out_specs=vmem,
+        scratch_shapes=[
+            pltpu.VMEM((PARTS, part_len, query_cols), bf16),
+            pltpu.VMEM((PARTS, 2 * key_cols, part_len), bf16),
+            pltpu.VMEM((PARTS, 16, head_size, out_cols), bf16),
+            pltpu.VMEM((slot_count, head_size), bf16),
+            pltpu.VMEM((slot_count, head_size), bf16),
+            pltpu.VMEM((PARTS, PEERS, 48, width), bf16),
+            pltpu.VMEM((48, part_len), bf16),
+            pltpu.VMEM((3, PEERS * 16, 128), f32),
+            pltpu.VMEM((PEERS * 32, 128), f32),
+            pltpu.VMEM((48, query_cols), f32),
+            pltpu.VMEM((48, out_cols), f32),
+            pltpu.VMEM((3, 48, head_size), bf16),
+            pltpu.VMEM((PEERS, 16, head_size), bf16),
+            pltpu.VMEM((PEERS, 16, head_size), bf16),
+            pltpu.VMEM((PEERS, 32, 128), bf16),
+            pltpu.VMEM((PEERS, 32, 128), bf16),
+            dma((PARTS,)),
+            dma((PARTS, 2)),
+            dma((PARTS,)),
+            dma((2,)),
+            dma((PARTS, 6)),
+            dma((PARTS, 2, PEERS)),
+            dma((PARTS, PEERS)),
+            dma((PEERS,)),
+            dma((PEERS,)),
+            dma((PEERS,)),
+            dma((PEERS,)),
+        ],
+        compiler_params=pltpu.CompilerParams(
+            collective_id=0, has_side_effects=True, vmem_limit_bytes=VMEM_BYTES
+        ),
+    )(
+        tokens.reshape(step_count, model_width),
+        gain.reshape(1, model_width),
+        lengths,
+        positions,
+        w_query.reshape(PARTS, part_len, query_cols),
+        w_key.T,
+        w_value.T,
+        w_out.reshape(16, PARTS, head_size, out_cols),
+        cache_keys.reshape(slot_count, head_size),
+        cache_values.reshape(slot_count, head_size),
+    )
+    return result.reshape(step_count, 1, model_width)
+
+
 def solution(mesh):
     in_specs = (
         P(None, ("groups", "gx"), None),
@@ -122,5 +628,5 @@
     )
     out_specs = P(None, ("groups", "gx"), None)
     return jax.shard_map(
-        per_device, mesh=mesh, in_specs=in_specs, out_specs=out_specs, check_vma=False
-    )
+        layer, mesh=mesh, in_specs=in_specs, out_specs=out_specs, check_vma=False
+    )

time: 160 us -> 65.6 us (0.41)
  waiting for transfers between devices: 88.5 us -> 0 us
  Pallas kernels: 0 us -> 62.5 us
  matrix products: 34.4 us -> 0 us
  between operations: 14.9 us -> 1.3 us
  blocking collectives: 11.6 us -> 0 us
  other arithmetic: 3.89 us -> 0 us
  starting transfers between devices: 3.74 us -> 0 us
    all_gather x2 -> x0, waiting for transfers between devices: 81.8 us -> none  [the longest x1 44.4 us: per_device(): everyone = lax.all_gather(normed, 'gx', axis=1, tiled=True)]
    pallas_call x0 -> x1, Pallas kernels: none -> 62.5 us  [layer(): pl.pallas_call(layer_kernel, out_shape=jax.ShapeDtypeStruct((step_count,...]
    dot_general x8 -> x0, matrix products: 34.4 us -> none  [the longest x3 18.3 us: project(): jnp.einsum('cbd,de->cbe', everyone, weight, preferred_element_type=jnp.fl...]
    all_to_all x1 -> x0, blocking collectives: 11.6 us -> none  [per_device(): lax.all_to_all(mixed_cols, 'gx', split_axis=1, concat_axis=2, tiled=True)]
    all_to_all x1 -> x0, waiting for transfers between devices: 6.75 us -> none  [per_device(): lax.all_to_all(together.reshape(step_count, devices, row_count, -1), 'gx'...]
    all_to_all x1 -> x0, starting transfers between devices: 3.51 us -> none  [per_device(): lax.all_to_all(together.reshape(step_count, devices, row_count, -1), 'gx'...]
    convert_element_type x2 -> x0, other arithmetic: 1.8 us -> none  [the longest x1 1.79 us: per_device(): ((row_mean_input - row_mean) * lax.rsqrt(row_spread + 1e-06) * gain).asty...]
    reduce_sum x3 -> x0, other arithmetic: 1.63 us -> none  [the longest x1 1.29 us: per_device(): row_mean = jnp.mean(row_mean_input, axis=-1, keepdims=True)]
  transfers between devices with their start and end apart: 3 -> 0, of which waited for: 3 -> 0; matrix products, arithmetic and copies ran while one was open for 0% -> 0% of each run, Pallas kernels for 0% -> 0%
where the time goes in v1:
time: 65.6 us; the launch traced here: 65.4 us
  Pallas kernels  62.5 us (95%)
  local copies, waits for them, and re-layouts  1.62 us (2%)
  between operations  1.3 us (2%)
    pallas_call x1, Pallas kernels, layer(): pl.pallas_call(layer_kernel, out_shape=jax.ShapeDtypeStruct((step_count,...  62.5 us
    unnamed x1, local copies, waits for them, and re-layouts  1.62 us

profile of v1, /device:TPU:0, one launch (start us, length us, event | category | flops | bytes accessed | tf_op | source)
XLA Modules:
  0.0 65.4 jit_solution(4775945055560357062)
XLA Ops:
  1.3 62.5 %shard_map.100 = bf16[3,18432]{1,0:T(4,128)(2,1)} custom-call(bf16[3,18432]{1,0:T(4,128)(2,1)} %bitcast.16, f32[1,18432]{1,0:T(1,128)} %bitcast.17, s32[1]{0:T(128)S(6)} %copy.12.lengths, s32[1]{0:T(128)S(6)} %copy.13.positions, bf16[3,6144,768]{2,1,0:T(8,128)(2,1)} %bitcast.9, bf16[16,18432]{1,0:T(8,128)(2,1)} %bitcast.13, bf16[16,18432]{1,0:T(8,128)(2,1)} %bitcast.14, ...), custom_call_target="tpu_custom_call" | custom-call | tf_op jit(solution)/shard_map/pallas_call | solution.py:564
  63.8 1.6 %copy.14 = bf16[3,1,18432]{2,0,1:T(4,128)(2,1)} copy(bf16[3,1,18432]{2,0,1:T(4,128)(2,1)} %bitcast.15) | data formatting | bytes 221184
